TPU v7x, 32 devices: a whole 2x2x4 slice. The times are simulated.
32 devices in a mesh: groups: 2 (over y), tensor: 4 (over z), expert: 4 (over x, core).
Axes of the slice: x: 2, y: 2, z: 4, core: 2. Of those that a mesh axis runs over, the one named last changes fastest.
Arguments:
- tokens: bfloat16 [1024, 3072], P(('groups', 'expert'), 'tensor'), parts along dimension 0, may hold values from -6 to 6
- routes: int32 [1024, 2], P(('groups', 'expert')), parts along dimension 0, may hold values from 0 to 3, all different within a row; in each aligned block of 128 rows (0 to 127, 128 to 255, ...) at most 72 rows name the same one
- gates: float32 [1024, 2], P(('groups', 'expert')), parts along dimension 0, may hold values from 0.25 to 1
- w_gate: bfloat16 [4, 3072, 8192], P('expert', None, 'tensor'), may hold values from -0.109375 to 0.109375
- w_up: bfloat16 [4, 3072, 8192], P('expert', None, 'tensor'), may hold values from -0.109375 to 0.109375
- w_down: bfloat16 [4, 8192, 3072], P('expert', 'tensor'), may hold values from -0.09375 to 0.09375
Outputs:
- mixed: bfloat16 [1024, 3072], P(('groups', 'expert'), 'tensor'), parts along dimension 0
There are 2 independent parts, one for each index of `groups`. A program takes and returns all parts, laid end to end along the dimension named above; an argument that names none is the same for every part. Nothing has to cross between parts.
Inputs may be any that keep to these rules, and one draw needn't show every extreme that they name: `routes`: each row names two different experts. Among the rows of one index of expert no expert is named more than 72 times, a bound that some block reaches.
All inputs are finite; a program needn't handle non-finite values.
Results may differ from a plain program's by a relative error of at most 0.012.
Values may be sent and summed in bfloat16 or wider, within the bound.
A program may use at most 128 MiB of HBM per device.

v0:
```python
import jax
import jax.numpy as jnp
from jax import lax
from jax.sharding import PartitionSpec as P

CAP = 72


row_tile = 128


def route_ranks(flat, experts):
    onehot = (flat[:, None] == jnp.arange(experts, dtype=jnp.int32)[None, :]).astype(jnp.int32)
    return jnp.sum((jnp.cumsum(onehot, axis=0) - 1) * onehot, axis=1)


def tile_terms(block, gate_panel, up_panel, down_panel):
    gate = jnp.dot(block, gate_panel, preferred_element_type=jnp.float32)
    upper = jnp.dot(block, up_panel, preferred_element_type=jnp.float32)
    hidden = (jax.nn.silu(gate) * upper).astype(jnp.bfloat16)
    return jnp.dot(hidden, down_panel, preferred_element_type=jnp.float32)


def expert_rows(rows, live, gate_panel, up_panel, down_panel):
    total = rows.shape[0]
    width = down_panel.shape[1]

    def step(index, acc):
        block = lax.dynamic_slice_in_dim(rows, index * row_tile, row_tile, 0)
        product = tile_terms(block, gate_panel, up_panel, down_panel)
        return lax.dynamic_update_slice_in_dim(acc, product, index * row_tile, 0)

    tiles = (live + row_tile - 1) // row_tile
    return lax.fori_loop(0, tiles, step, jnp.zeros((total, width), jnp.float32))


def compact_rows(arrived, incoming, offsets, padded):
    experts, capacity, width = arrived.shape
    position = jnp.arange(experts * capacity, dtype=jnp.int32)
    source = position // capacity
    within = position % capacity
    live_row = within < incoming[source]
    dest = jnp.where(live_row, offsets[source] + within, padded)
    flat_rows = arrived.reshape(experts * capacity, width)
    return jnp.zeros((padded, width), arrived.dtype).at[dest].set(flat_rows, mode="drop")


def per_device(tokens, routes, gates, w_gate, w_up, w_down):
    experts = lax.axis_size("expert")
    me = lax.axis_index("expert")
    tok = routes.shape[0]
    slice_width = tokens.shape[1]
    slots = experts * CAP
    padded = (slots + row_tile - 1) // row_tile * row_tile
    table = lax.all_gather(routes, "expert", axis=0, tiled=True)
    every_flat = table.reshape(-1)
    source_of = jnp.arange(every_flat.shape[0], dtype=jnp.int32) // (2 * tok)
    pair_index = source_of * experts + every_flat
    loads = jnp.sum(
        (pair_index[:, None] == jnp.arange(experts * experts, dtype=jnp.int32)[None, :]).astype(
            jnp.int32
        ),
        axis=0,
    ).reshape(experts, experts)
    flat = routes.reshape(-1)
    ranks = route_ranks(flat, experts)
    token_of = jnp.arange(2 * tok, dtype=jnp.int32) // 2
    incoming = loads[:, me]
    offsets = jnp.cumsum(incoming) - incoming
    live = jnp.sum(incoming)
    target = flat * CAP + ranks
    chosen = tokens[token_of]
    width = chosen.shape[1]
    outgoing = (
        jnp.zeros((slots, width), jnp.bfloat16)
        .at[target]
        .set(chosen, mode="drop")
        .reshape(experts, CAP, width)
    )
    arrived = lax.all_to_all(outgoing, "expert", split_axis=0, concat_axis=0, tiled=True)
    stacked = compact_rows(arrived, incoming, offsets, padded)
    stacked = lax.all_gather(stacked, "tensor", axis=1, tiled=True)
    terms = expert_rows(stacked, live, w_gate[0], w_up[0], w_down[0])
    summed = lax.psum_scatter(terms.astype(jnp.bfloat16), "tensor", scatter_dimension=1, tiled=True)
    position = jnp.arange(slots, dtype=jnp.int32)
    source = position // CAP
    within = position % CAP
    live_row = within < incoming[source]
    fetch = jnp.clip(offsets[source] + within, 0, padded - 1)
    restored = jnp.where(
        live_row[:, None], summed[fetch], jnp.zeros((slots, slice_width), jnp.bfloat16)
    )
    returned = lax.all_to_all(
        restored.reshape(experts, CAP, slice_width),
        "expert",
        split_axis=0,
        concat_axis=0,
        tiled=True,
    ).reshape(slots, slice_width)
    picked = returned[jnp.clip(target, 0, slots - 1)]
    weighted = picked.astype(jnp.float32).reshape(tok, 2, slice_width) * gates[:, :, None]
    return jnp.sum(weighted, axis=1).astype(jnp.bfloat16)


def solution(mesh):
    in_specs = (
        P(("groups", "expert"), "tensor"),
        P(("groups", "expert"), None),
        P(("groups", "expert"), None),
        P("expert", None, "tensor"),
        P("expert", None, "tensor"),
        P("expert", "tensor", None),
    )
    out_specs = P(("groups", "expert"), "tensor")
    return jax.shard_map(
        per_device, mesh=mesh, in_specs=in_specs, out_specs=out_specs, check_vma=False
    )
```

profile of v0, /device:TPU:0, one launch (start us, length us, event | category | flops | bytes accessed | tf_op | source)
XLA Modules:
  0.0 222.3 jit_solution(15529719609317617772)
XLA Ops:
  6.5 0.0 copy-start
  6.5 0.8 copy.19
  7.4 0.1 eq.48
  7.5 0.1 eq.44
  7.6 0.7 broadcast_multiply_fusion
  8.4 1.2 reduce-window.20
  9.6 0.1 slice.33
  9.7 0.1 copy.21
  9.8 0.1 copy.22
  9.9 0.1 add_bitcast_fusion
  10.0 0.1 copy.18
  10.1 0.1 mul.56
  10.3 0.0 copy-done
  10.3 3.9 %scatter_custom_fusion = bf16[288,768]{1,0:T(8,128)(2,1)} fusion(s32[256]{0:T(256)S(1)} %bitcast.51, bf16[128,768]{1,0:T(8,128)(2,1)S(1)} %copy-done, s32[1024]{0:T(1024)S(1)} %pad_clamp_fusion.2, bf16[]{:T(256)} %constant.113.clone.1), kind=kCustom, calls=%fused_computation.17 | custom fusion | bytes 442370 | tf_op jit(solution)/shard_map/scatter | solution.py:77
  14.1 4.2 %all-to-all-start = ((bf16[4,72,768]{2,1,0:T(8,128)(2,1)}), bf16[4,72,768]{2,1,0:T(8,128)(2,1)S(1)}, u32[]{:S(2)}, u32[]{:S(2)}) async-start(bf16[4,72,768]{2,1,0:T(8,128)(2,1)} %bitcast.13), calls=%async_computation | async-start | bytes 884736 | tf_op jit(solution)/shard_map/all_to_all | solution.py:80
  18.3 0.0 all-gather.2.cloned.1.call-start
  18.3 8.8 %all_gather.6 = s32[512,2]{0,1:T(2,128)S(1)} all-gather(s32[128,2]{0,1:T(2,128)} %param.9), channel_id=1, replica_groups=mesh['groups'=2,'tensor'=4,'expert'=4] {'expert'}, dimensions={0}, use_global_device_ids=true | all-gather | bytes 5120 | tf_op jit(solution)/shard_map/all_gather | solution.py:55
  27.2 0.1 copy.17
  27.3 0.2 reshape.282
  27.5 0.1 convert_reduce_fusion
  27.7 0.1 reshape.283
  27.7 0.7 fusion.31
  28.5 0.6 fusion.32
  29.1 0.6 fusion.33
  29.7 5.0 %fusion.28 = s32[288]{0:T(512)S(1)} fusion(s32[]{:T(128)} %bitcast.7, s32[]{:T(128)} %bitcast.6, s32[]{:T(128)} %bitcast.5, s32[]{:T(128)} %bitcast.4, s32[]{:T(128)} %bitcast.3, s32[]{:T(128)} %bitcast.2, s32[]{:T(128)} %bitcast.1, s32[]{:T(128)} %bitcast), kind=kLoop, calls=%fused_computation.70 | loop fusion | flops 8640 | bytes 1184 | tf_op jit(solution)/shard_map/select_n | solution.py:45
  34.6 0.0 all-to-all-done
  34.6 2.6 %scatter_custom_fusion.1 = bf16[384,768]{1,0:T(8,128)(2,1)} fusion(s32[288]{0:T(512)S(1)} %fusion.28, bf16[288,768]{1,0:T(8,128)(2,1)S(1)} %bitcast.46, bf16[]{:T(256)} %constant.113.clone.1), kind=kCustom, calls=%fused_computation.19 | custom fusion | bytes 589826 | tf_op jit(solution)/shard_map/scatter | solution.py:45
  37.2 0.0 all-gather.2.cloned.1.call-update
  37.3 0.0 reduce-scatter.2.cloned.1.call-start
  38.0 50.9 %all-gather.2.cloned.1.call-done = bf16[384,3072]{1,0:T(8,128)(2,1)} async-done(((bf16[384,768]{1,0:T(8,128)(2,1)}), bf16[384,3072]{1,0:T(8,128)(2,1)}) %all-gather.2.cloned.1.call-update) | async-done | bytes 2359312 | tf_op jit(solution)/shard_map/all_gather | solution.py:82
  88.9 1.7 broadcast_in_dim.14
  90.6 39.2 %while.10 = (s32[]{:T(128)}, bf16[384,3072]{1,0:T(8,128)(2,1)}, s32[]{:T(128)}, bf16[384,3072]{1,0:T(8,128)(2,1)}, bf16[3072,2048]{1,0:T(8,128)(2,1)}, /*index=5...) while((s32[]{:T(128)}, bf16[384,3072]{1,0:T(8,128)(2,1)}, ...), condition=%wide.region_9.10_spmd, body=%wide.region_8.9_spmd.sunk | while | flops 4833411072 | bytes 42992800 | solution.py:34
  90.6 6.6 %fusion.48 = f32[128,2048]{1,0:T(8,128)S(1)} fusion(bf16[3072,2048]{1,0:T(8,128)(2,1)} %get-tuple-element.140, bf16[384,3072]{1,0:T(8,128)(2,1)} %get-tuple-element.139, s32[]{:T(128)S(6)} %select_n.232), kind=kOutput, calls=%fused_computation.9.clone.1 | convolution fusion | flops 1610612736 | bytes 14417924 | tf_op jit(solution)/shard_map/while/body/dot_general | solution.py:18
  97.2 13.0 %convolution_dynamic-update-slice_fusion.2 = bf16[384,3072]{1,0:T(8,128)(2,1)} fusion(bf16[384,3072]{1,0:T(8,128)(2,1)} %get-tuple-element.126, s32[]{:T(128)S(6)} %select_n.232, bf16[2048,3072]{1,0:T(8,128)(2,1)} %get-tuple-element.142, bf16[3072,2048]{1,0:T(8,128)(2,1)} %get-tuple-element.141, f32[128,2048]{1,0:T(8,128)S(1)} %fusion.48, ...), kind=kOutput, calls=%fused_computation.5.clone.1 | convolution fusion | flops 3222798336 | bytes 28574720 | tf_op jit(solution)/shard_map/while/body/dot_general | solution.py:21
  110.2 6.6 %fusion.48 = f32[128,2048]{1,0:T(8,128)S(1)} fusion(bf16[3072,2048]{1,0:T(8,128)(2,1)} %get-tuple-element.140, bf16[384,3072]{1,0:T(8,128)(2,1)} %get-tuple-element.139, s32[]{:T(128)S(6)} %select_n.232), kind=kOutput, calls=%fused_computation.9.clone.1 | convolution fusion | flops 1610612736 | bytes 14417924 | tf_op jit(solution)/shard_map/while/body/dot_general | solution.py:18
  116.8 12.9 %convolution_dynamic-update-slice_fusion.2 = bf16[384,3072]{1,0:T(8,128)(2,1)} fusion(bf16[384,3072]{1,0:T(8,128)(2,1)} %get-tuple-element.126, s32[]{:T(128)S(6)} %select_n.232, bf16[2048,3072]{1,0:T(8,128)(2,1)} %get-tuple-element.142, bf16[3072,2048]{1,0:T(8,128)(2,1)} %get-tuple-element.141, f32[128,2048]{1,0:T(8,128)S(1)} %fusion.48, ...), kind=kOutput, calls=%fused_computation.5.clone.1 | convolution fusion | flops 3222798336 | bytes 28574720 | tf_op jit(solution)/shard_map/while/body/dot_general | solution.py:21
  129.7 0.0 reduce-scatter.2.cloned.1.call-update
  129.7 2.5 %fusion.30 = s32[288]{0:T(512)S(1)} fusion(s32[]{:T(128)} %bitcast.3, s32[]{:T(128)} %bitcast.2, s32[]{:T(128)} %bitcast.1, s32[]{:T(128)} %bitcast), kind=kLoop, calls=%fused_computation.73 | loop fusion | flops 4896 | bytes 1168 | tf_op jit(solution)/shard_map/gather | solution.py:88
  132.3 0.1 gather.26
  132.4 2.4 %fusion.29 = s32[288]{0:T(512)S(1)} fusion(s32[]{:T(128)} %bitcast.7, s32[]{:T(128)} %bitcast.6, s32[]{:T(128)} %bitcast.5, s32[]{:T(128)} %bitcast.4), kind=kLoop, calls=%fused_computation.71 | loop fusion | flops 7488 | bytes 1168 | tf_op jit(solution)/shard_map/select_n | solution.py:91
  134.8 0.0 copy-start.1
  134.9 61.4 %reduce-scatter.2.cloned.1.call-done = bf16[384,768]{1,0:T(8,128)(2,1)} async-done(((bf16[384,3072]{1,0:T(8,128)(2,1)}), bf16[384,768]{1,0:T(8,128)(2,1)}) %reduce-scatter.2.cloned.1.call-update) | async-done | bytes 589840 | tf_op jit(solution)/shard_map/reduce_scatter | solution.py:84
  196.3 3.6 %gather_fusion = bf16[288,768]{1,0:T(8,128)(2,1)S(1)} fusion(bf16[384,768]{1,0:T(8,128)(2,1)} %reduce-scatter.2.cloned.1.call-done, s32[1024]{0:T(1024)S(1)} %pad_clamp_fusion.1), kind=kCustom, calls=%fused_computation.1 | custom fusion | bytes 885888 | tf_op jit(solution)/shard_map/gather | solution.py:91
  199.9 0.9 broadcast_select_fusion
  200.8 3.5 %all-to-all-start.1 = ((bf16[4,72,768]{2,1,0:T(8,128)(2,1)}), bf16[4,72,768]{2,1,0:T(8,128)(2,1)S(1)}, u32[]{:S(2)}, u32[]{:S(2)}) async-start(bf16[4,72,768]{2,1,0:T(8,128)(2,1)} %broadcast_select_fusion), calls=%async_computation.2 | async-start | bytes 884736 | tf_op jit(solution)/shard_map/all_to_all | solution.py:93
  204.3 0.0 copy-done.1
  204.3 0.1 copy.23
  204.4 7.8 %all-to-all-done.1 = bf16[4,72,768]{2,1,0:T(8,128)(2,1)S(1)} async-done(((bf16[4,72,768]{2,1,0:T(8,128)(2,1)}), bf16[4,72,768]{2,1,0:T(8,128)(2,1)S(1)}, u32[]{:S(2)}, u32[]{:S(2)}) %all-to-all-start.1) | async-done | bytes 442400 | tf_op jit(solution)/shard_map/all_to_all | solution.py:93
  212.2 1.2 gather_fusion.1
  213.4 0.4 reshape.289
  213.8 1.7 multiply_reduce_fusion
  (13 shorter events, 0.2 us)
Async XLA Ops:
  6.5 3.7 %copy-start = (bf16[128,768]{1,0:T(8,128)(2,1)S(1)}, bf16[128,768]{1,0:T(8,128)(2,1)}, u32[]{:S(2)}) copy-start(bf16[128,768]{1,0:T(8,128)(2,1)} %param.8) | copy-start | bytes 589828
  14.1 20.5 %all-to-all-start = ((bf16[4,72,768]{2,1,0:T(8,128)(2,1)}), bf16[4,72,768]{2,1,0:T(8,128)(2,1)S(1)}, u32[]{:S(2)}, u32[]{:S(2)}) async-start(bf16[4,72,768]{2,1,0:T(8,128)(2,1)} %bitcast.13), calls=%async_computation | async-start | bytes 884736 | tf_op jit(solution)/shard_map/all_to_all | solution.py:80
  18.3 70.5 %all-gather.2.cloned.1.call-start = ((), (), s32[]{:S(2)}) async-start(), calls=%async_computation.3 | async-start | bytes 2949120 | tf_op jit(solution)/shard_map/all_gather | solution.py:82
  37.3 159.0 %reduce-scatter.2.cloned.1.call-start = ((), (), s32[]{:S(2)}) async-start(), calls=%async_computation.4 | async-start | bytes 2949120 | tf_op jit(solution)/shard_map/reduce_scatter | solution.py:84
  134.8 69.4 %copy-start.1 = (f32[128,2]{0,1:T(2,128)S(1)}, f32[128,2]{0,1:T(2,128)}, u32[]{:S(2)}) copy-start(f32[128,2]{0,1:T(2,128)} %param.10) | copy-start | bytes 3076
  200.8 11.4 %all-to-all-start.1 = ((bf16[4,72,768]{2,1,0:T(8,128)(2,1)}), bf16[4,72,768]{2,1,0:T(8,128)(2,1)S(1)}, u32[]{:S(2)}, u32[]{:S(2)}) async-start(bf16[4,72,768]{2,1,0:T(8,128)(2,1)} %broadcast_select_fusion), calls=%async_computation.2 | async-start | bytes 884736 | tf_op jit(solution)/shard_map/all_to_all | solution.py:93
Sparse Core Ops, SparseCore 0:
  37.4 51.4 all-gather.1
  129.9 66.3 reduce-scatter.1
where the time goes:
time: 223 us; the launch traced here: 222 us
  waiting for transfers between devices  120 us (54%)
  matrix products  39.1 us (18%)
  local copies, waits for them, and re-layouts  16.7 us (7%)
  other arithmetic  15.5 us (7%)
  between operations  14.2 us (6%)
  blocking collectives  8.85 us (4%)
  starting transfers between devices  7.71 us (3%)
    reduce_scatter x1, waiting for transfers between devices, per_device(): lax.psum_scatter(terms.astype(jnp.bfloat16), 'tensor', scatter_dimension=...  61.4 us
    all_gather x1, waiting for transfers between devices, per_device(): stacked = lax.all_gather(stacked, 'tensor', axis=1, tiled=True)  50.9 us
    dot_general x2, matrix products, tile_terms(): return jnp.dot(hidden, down_panel, preferred_element_type=jnp.float32)  25.9 us
    dot_general x2, matrix products, tile_terms(): gate = jnp.dot(block, gate_panel, preferred_element_type=jnp.float32)  13.3 us
    all_gather x1, blocking collectives, per_device(): table = lax.all_gather(routes, 'expert', axis=0, tiled=True)  8.85 us
    all_to_all x1, waiting for transfers between devices, per_device(): lax.all_to_all(restored.reshape(experts, CAP, slice_width), 'expert', spl...  7.8 us
    select_n x1, other arithmetic, compact_rows(): jnp.zeros((padded, width), arrived.dtype).at[dest]  4.95 us
  transfers between devices with their start and end apart: 4, of which 3 were waited for; matrix products, arithmetic and copies ran while one was open for 6% of the time, Pallas kernels for 0%

commit v1 on v0

--- a/solution.py
+++ b/solution.py
@@ -1,9 +1,12 @@
 import jax
 import jax.numpy as jnp
 from jax import lax
+from jax.experimental import pallas as pl
+from jax.experimental.pallas import tpu as pltpu
 from jax.sharding import PartitionSpec as P
 
 CAP = 72
+MESH = pl.DeviceIdType.MESH
 
 
 row_tile = 128
@@ -102,6 +105,270 @@
     return jnp.sum(weighted, axis=1).astype(jnp.bfloat16)
 
 
+def pair_steps(z):
+    return (z, z + 1 - 2 * (z % 2), (z + 2) % 4, 3 - z)
+
+
+def layer_kernel(
+    meta_in, tok_in, gate_hbm, up_hbm, down_hbm, out,
+    toks, meta, gate_w, up_w, down_w, gate_acc, up_acc, rows_buf, hid, pick, place, scale, terms,
+    outs, core_in, x_out, x_in, z_out, z_in,
+    w_sem, meta_send, meta_recv, z_send, x_send, core_send, tok_recv,
+    rc_send, rc_recv, rx_send, rx_recv, rz_send, rz_recv,
+):
+    e = lax.axis_index("expert")
+    z = lax.axis_index("tensor")
+    x = e // 2
+    c = e % 2
+    core_e = 2 * x + 1 - c
+    x_e = 2 * (1 - x) + c
+    diag_e = 2 * (1 - x) + 1 - c
+    zs = pair_steps(z)
+    tok, width = tok_in.shape
+    slots = pick.shape[0]
+    every = pick.shape[1]
+    hidden = hid.shape[1]
+
+    weight_copies = []
+    for k in range(4):
+        cut = pl.ds(pl.multiple_of(zs[k] * width, width), width)
+        weight_copies.append(
+            (
+                pltpu.make_async_copy(gate_hbm.at[cut, :], gate_w.at[k], w_sem.at[k]),
+                pltpu.make_async_copy(up_hbm.at[cut, :], up_w.at[k], w_sem.at[4 + k]),
+                pltpu.make_async_copy(down_hbm.at[:, cut], down_w.at[k], w_sem.at[8 + k]),
+            )
+        )
+    for k in range(4):
+        weight_copies[k][0].start()
+        weight_copies[k][1].start()
+    for k in (3, 2, 1, 0):
+        weight_copies[k][2].start()
+
+    barrier = pltpu.get_barrier_semaphore()
+    for other in (core_e, x_e, diag_e):
+        pl.semaphore_signal(barrier, inc=1, device_id={"expert": other}, device_id_type=MESH)
+    for k in (1, 2, 3):
+        pl.semaphore_signal(barrier, inc=1, device_id={"tensor": zs[k]}, device_id_type=MESH)
+    pl.semaphore_wait(barrier, 6)
+
+    sends = []
+
+    def send(src, dst, s_sem, r_sem, where):
+        copy = pltpu.make_async_remote_copy(
+            src_ref=src, dst_ref=dst, send_sem=s_sem, recv_sem=r_sem,
+            device_id=where, device_id_type=MESH,
+        )
+        copy.start()
+        sends.append(copy)
+
+    def arrival(ref, sem):
+        pltpu.make_async_copy(ref, ref, sem).wait()
+
+    for i, other in enumerate((x_e, core_e, diag_e)):
+        send(meta_in, meta.at[e], meta_send.at[i], meta_recv.at[e], {"expert": other})
+    own = z * 4 + e
+    send(tok_in, toks.at[own], x_send.at[0], tok_recv.at[own], {"expert": x_e})
+    for k in (1, 2, 3):
+        send(tok_in, toks.at[own], z_send.at[k - 1], tok_recv.at[own], {"tensor": zs[k]})
+    send(tok_in, toks.at[own], core_send.at[0], tok_recv.at[own], {"expert": core_e})
+    toks[own] = tok_in[...]
+    meta[e] = meta_in[...]
+
+    def forward_z(k):
+        block = zs[k] * 4 + e
+        arrival(toks.at[block], tok_recv.at[block])
+        send(toks.at[block], toks.at[block], x_send.at[k], tok_recv.at[block], {"expert": x_e})
+        send(toks.at[block], toks.at[block], core_send.at[k], tok_recv.at[block], {"expert": core_e})
+
+    def forward_x(k):
+        block = zs[k] * 4 + x_e
+        arrival(toks.at[block], tok_recv.at[block])
+        send(toks.at[block], toks.at[block], core_send.at[4 + k], tok_recv.at[block], {"expert": core_e})
+
+    for other in (x_e, core_e, diag_e):
+        arrival(meta.at[other], meta_recv.at[other])
+
+    own_row = lax.broadcasted_iota(jnp.int32, (8, tok), 0) == e
+    weight = jnp.concatenate(
+        [jnp.sum(jnp.where(own_row, meta[s], 0.0), axis=0, keepdims=True) for s in range(4)], axis=1
+    )
+    live = weight > 0.0
+    ones = jnp.broadcast_to(jnp.where(live, 1.0, 0.0), (16, every)).astype(jnp.bfloat16)
+    before = jnp.where(
+        lax.broadcasted_iota(jnp.int32, (every, every), 0)
+        < lax.broadcasted_iota(jnp.int32, (every, every), 1),
+        1.0,
+        0.0,
+    ).astype(jnp.bfloat16)
+    rank = jnp.dot(ones, before, preferred_element_type=jnp.float32)[0:1]
+    key = jnp.where(live, rank, -1.0)
+    row_hit = lax.broadcasted_iota(jnp.int32, (slots, every), 0).astype(jnp.float32) == key
+    pick[...] = jnp.where(row_hit, 1.0, 0.0).astype(jnp.bfloat16)
+    scale[...] = jnp.broadcast_to(
+        jnp.sum(jnp.where(row_hit, weight, 0.0), axis=1, keepdims=True), scale.shape
+    )
+    column = jnp.transpose(jnp.broadcast_to(key, (128, every)))[:, 0:1]
+    padded = place.shape[1]
+    place[...] = jnp.where(
+        lax.broadcasted_iota(jnp.int32, (every, padded), 1).astype(jnp.float32) == column, 1.0, 0.0
+    ).astype(jnp.bfloat16)
+    terms[slots:, :] = jnp.zeros((padded - slots, width), jnp.bfloat16)
+
+    tile = 512
+
+    def up_step(k):
+        weight_copies[k][0].wait()
+        weight_copies[k][1].wait()
+        blocks = toks[pl.ds(zs[k] * 4, 4)].reshape(every, width)
+        rows_buf[...] = jnp.dot(
+            pick[...], blocks, preferred_element_type=jnp.float32
+        ).astype(jnp.bfloat16)
+
+        @pl.loop(0, hidden // tile)
+        def _(i):
+            cols = pl.ds(pl.multiple_of(i * tile, tile), tile)
+            rows = rows_buf[...]
+            gate = jnp.dot(rows, gate_w[k, :, cols], preferred_element_type=jnp.float32)
+            upper = jnp.dot(rows, up_w[k, :, cols], preferred_element_type=jnp.float32)
+            if k > 0:
+                gate = gate + gate_acc[:, cols]
+                upper = upper + up_acc[:, cols]
+            if k < 3:
+                gate_acc[:, cols] = gate
+                up_acc[:, cols] = upper
+            else:
+                hid[:, cols] = (gate / (1.0 + jnp.exp(-gate)) * upper).astype(jnp.bfloat16)
+
+    def core_arrivals(k):
+        for other in (core_e, diag_e):
+            block = zs[k] * 4 + other
+            arrival(toks.at[block], tok_recv.at[block])
+
+    for k in range(4):
+        if k < 3:
+            forward_z(k + 1)
+        forward_x(k)
+        core_arrivals(k)
+        up_step(k)
+
+    down_tile = 256
+
+    def down_step(k):
+        weight_copies[k][2].wait()
+
+        @pl.loop(0, width // down_tile)
+        def _(i):
+            cols = pl.ds(pl.multiple_of(i * down_tile, down_tile), down_tile)
+            product = jnp.dot(hid[...], down_w[k, :, cols], preferred_element_type=jnp.float32)
+            terms[0:slots, cols] = (product * scale[:, 0:1]).astype(jnp.bfloat16)
+            spread = jnp.dot(place[...], terms[:, cols], preferred_element_type=jnp.float32)
+            outs[k, :, :, cols] = spread.astype(jnp.bfloat16).reshape(4, tok, down_tile)
+
+        for i, there in enumerate((1 - x, x)):
+            send(
+                outs.at[k, 2 * there + 1 - c], core_in.at[k, i],
+                rc_send.at[2 * k + i], rc_recv.at[2 * k + i], {"expert": core_e},
+            )
+
+    def core_step(k):
+        arrival(core_in.at[k, 0], rc_recv.at[2 * k])
+        x_out[k] = (
+            outs[k, x_e].astype(jnp.float32) + core_in[k, 0].astype(jnp.float32)
+        ).astype(jnp.bfloat16)
+        send(x_out.at[k], x_in.at[k], rx_send.at[k], rx_recv.at[k], {"expert": x_e})
+
+    def x_step(k):
+        arrival(core_in.at[k, 1], rc_recv.at[2 * k + 1])
+        arrival(x_in.at[k], rx_recv.at[k])
+        total = (
+            outs[k, e].astype(jnp.float32)
+            + core_in[k, 1].astype(jnp.float32)
+            + x_in[k].astype(jnp.float32)
+        )
+        if k > 0:
+            z_out[k - 1] = total.astype(jnp.bfloat16)
+            send(
+                z_out.at[k - 1], z_in.at[k - 1], rz_send.at[k - 1], rz_recv.at[k - 1],
+                {"tensor": zs[k]},
+            )
+            return None
+        return total
+
+    down_step(3)
+    core_step(3)
+    down_step(2)
+    core_step(2)
+    x_step(3)
+    down_step(1)
+    core_step(1)
+    down_step(0)
+    core_step(0)
+    x_step(2)
+    x_step(1)
+    total = x_step(0)
+    for k in (3, 2, 1):
+        arrival(z_in.at[k - 1], rz_recv.at[k - 1])
+        total = total + z_in[k - 1].astype(jnp.float32)
+    out[...] = total.astype(jnp.bfloat16)
+    for copy in sends:
+        copy.wait_send()
+
+
+def per_device_fused(tokens, routes, gates, w_gate, w_up, w_down):
+    tok, width = tokens.shape
+    model, hidden = w_gate.shape[1:]
+    experts = lax.axis_size("expert")
+    slots = experts * CAP
+    padded = (slots + 127) // 128 * 128
+    every = experts * tok
+    named = jnp.arange(8, dtype=jnp.int32)[:, None]
+    meta = jnp.where(routes[:, 0][None] == named, gates[:, 0][None], 0.0) + jnp.where(
+        routes[:, 1][None] == named, gates[:, 1][None], 0.0
+    )
+    vmem = pl.BlockSpec(memory_space=pltpu.VMEM)
+    hbm = pl.BlockSpec(memory_space=pl.ANY)
+    bf, f32, dma = jnp.bfloat16, jnp.float32, pltpu.SemaphoreType.DMA
+    return pl.pallas_call(
+        layer_kernel,
+        out_shape=jax.ShapeDtypeStruct((tok, width), bf),
+        in_specs=[vmem, vmem, hbm, hbm, hbm],
+        out_specs=vmem,
+        scratch_shapes=[
+            pltpu.VMEM((4 * experts, tok, width), bf),
+            pltpu.VMEM((experts, 8, tok), f32),
+            pltpu.VMEM((4, width, hidden), bf),
+            pltpu.VMEM((4, width, hidden), bf),
+            pltpu.VMEM((4, hidden, width), bf),
+            pltpu.VMEM((slots, hidden), f32),
+            pltpu.VMEM((slots, hidden), f32),
+            pltpu.VMEM((slots, width), bf),
+            pltpu.VMEM((slots, hidden), bf),
+            pltpu.VMEM((slots, every), bf),
+            pltpu.VMEM((every, padded), bf),
+            pltpu.VMEM((slots, 128), f32),
+            pltpu.VMEM((padded, width), bf),
+            pltpu.VMEM((4, experts, tok, width), bf),
+            pltpu.VMEM((4, 2, tok, width), bf),
+            pltpu.VMEM((4, tok, width), bf),
+            pltpu.VMEM((4, tok, width), bf),
+            pltpu.VMEM((3, tok, width), bf),
+            pltpu.VMEM((3, tok, width), bf),
+            dma((12,)), dma((3,)), dma((experts,)), dma((3,)), dma((4,)), dma((8,)),
+            dma((4 * experts,)),
+            dma((8,)), dma((8,)), dma((4,)), dma((4,)), dma((3,)), dma((3,)),
+        ],
+        compiler_params=pltpu.CompilerParams(
+            collective_id=0, has_side_effects=True, vmem_limit_bytes=62 * 1024 * 1024
+        ),
+        cost_estimate=pl.CostEstimate(
+            flops=6 * slots * model * hidden,
+            bytes_accessed=6 * model * hidden,
+            transcendentals=slots * hidden,
+        ),
+    )(meta, tokens, w_gate[0], w_up[0], w_down[0])
+
+
 def solution(mesh):
     in_specs = (
         P(("groups", "expert"), "tensor"),
@@ -112,6 +379,8 @@
         P("expert", "tensor", None),
     )
     out_specs = P(("groups", "expert"), "tensor")
+    fused = mesh.shape["tensor"] == 4 and mesh.shape["expert"] == 4
     return jax.shard_map(
-        per_device, mesh=mesh, in_specs=in_specs, out_specs=out_specs, check_vma=False
-    )
+        per_device_fused if fused else per_device,
+        mesh=mesh, in_specs=in_specs, out_specs=out_specs, check_vma=False,
+    )

time: 223 us -> 68.6 us (0.31)
  waiting for transfers between devices: 120 us -> 0 us
  Pallas kernels: 0 us -> 64.6 us
  matrix products: 39.1 us -> 0 us
  other arithmetic: 15.5 us -> 0.6 us
  between operations: 14.2 us -> 0.01 us
  local copies, waits for them, and re-layouts: 16.7 us -> 3.13 us
  blocking collectives: 8.85 us -> 0 us
  starting transfers between devices: 7.71 us -> 0 us
    pallas_call x0 -> x1, Pallas kernels: none -> 64.6 us  [per_device_fused(): pl.pallas_call(layer_kernel, out_shape=jax.ShapeDtypeStruct((tok, width),...]
    reduce_scatter x1 -> x0, waiting for transfers between devices: 61.4 us -> none  [per_device(): lax.psum_scatter(terms.astype(jnp.bfloat16), 'tensor', scatter_dimension=...]
    all_gather x1 -> x0, waiting for transfers between devices: 50.9 us -> none  [per_device(): stacked = lax.all_gather(stacked, 'tensor', axis=1, tiled=True)]
    dot_general x4 -> x0, matrix products: 39.1 us -> none  [the longest x2 25.9 us: tile_terms(): return jnp.dot(hidden, down_panel, preferred_element_type=jnp.float32)]
    all_gather x1 -> x0, blocking collectives: 8.85 us -> none  [per_device(): table = lax.all_gather(routes, 'expert', axis=0, tiled=True)]
    select_n x5 -> x0, other arithmetic: 8.3 us -> none  [the longest x1 4.95 us: compact_rows(): jnp.zeros((padded, width), arrived.dtype).at[dest]]
    all_to_all x2 -> x0, waiting for transfers between devices: 7.8 us -> none  [the longest x1 7.8 us: per_device(): lax.all_to_all(restored.reshape(experts, CAP, slice_width), 'expert', spl...]
    all_to_all x2 -> x0, starting transfers between devices: 7.67 us -> none  [the longest x1 4.21 us: per_device(): lax.all_to_all(outgoing, 'expert', split_axis=0, concat_axis=0, tiled=True)]
  transfers between devices with their start and end apart: 4 -> 0, of which waited for: 3 -> 0; matrix products, arithmetic and copies ran while one was open for 6% -> 0% of each run, Pallas kernels for 0% -> 0%
where the time goes in v1:
time: 68.6 us; the launch traced here: 68.3 us
  Pallas kernels  64.6 us (94%)
  local copies, waits for them, and re-layouts  3.13 us (5%)
    pallas_call x1, Pallas kernels, per_device_fused(): pl.pallas_call(layer_kernel, out_shape=jax.ShapeDtypeStruct((tok, width),...  64.6 us
    unnamed x1, local copies, waits for them, and re-layouts  1.62 us

profile of v1, /device:TPU:0, one launch (start us, length us, event | category | flops | bytes accessed | tf_op | source)
XLA Modules:
  0.0 68.3 jit_solution(16612683630117215074)
XLA Ops:
  0.0 0.8 %slice_bitcast_fusion.3 = (s32[128]{0:T(128)S(1)}, s32[128]{0:T(128)S(1)}) fusion(s32[128,2]{0,1:T(2,128)} %param.7), kind=kLoop, calls=%fused_computation.6 | loop fusion | bytes 2048 | tf_op jit(solution)/shard_map/eq | solution.py:326
  0.8 0.8 %slice_bitcast_fusion.2 = (f32[128]{0:T(128)S(1)}, f32[128]{0:T(128)S(1)}) fusion(f32[128,2]{0,1:T(2,128)} %param.8), kind=kLoop, calls=%fused_computation.5 | loop fusion | bytes 2048 | tf_op jit(solution)/shard_map/jit(_where)/broadcast_in_dim | solution.py:326
  1.5 0.6 select_add_fusion.meta_in
  2.1 64.6 %shard_map.64 = bf16[128,768]{1,0:T(8,128)(2,1)} custom-call(f32[8,128]{1,0:T(8,128)} %select_add_fusion.meta_in, bf16[128,768]{1,0:T(8,128)(2,1)} %tok_in.1, bf16[3072,2048]{1,0:T(8,128)(2,1)} %bitcast.11, bf16[3072,2048]{1,0:T(8,128)(2,1)} %bitcast.12, bf16[2048,3072]{1,0:T(8,128)(2,1)} %bitcast.13), custom_call_target="tpu_custom_call" | custom-call | flops 10871635968 | bytes 37748736 | tf_op jit(solution)/shard_map/pallas_call | solution.py:332
  66.7 1.6 %copy.8 = bf16[128,768]{1,0:T(8,128)(2,1)} copy(bf16[128,768]{1,0:T(8,128)(2,1)} %shard_map.64) | data formatting | bytes 393216

commit v2 on v1

--- a/solution.py
+++ b/solution.py
@@ -105,13 +105,14 @@
     return jnp.sum(weighted, axis=1).astype(jnp.bfloat16)
 
 
-def pair_steps(z):
-    return (z, z + 1 - 2 * (z % 2), (z + 2) % 4, 3 - z)
+def near_to_far(z):
+    half = z // 2
+    return (z, z + 1 - 2 * (z % 2), 2 - half, 3 - 3 * half)
 
 
 def layer_kernel(
-    meta_in, tok_in, gate_hbm, up_hbm, down_hbm, out,
-    toks, meta, gate_w, up_w, down_w, gate_acc, up_acc, rows_buf, hid, pick, place, scale, terms,
+    routes_in, gates_in, tok_in, gate_hbm, up_hbm, down_hbm, out,
+    toks, meta_in, meta, gate_w, up_w, down_w, gate_acc, up_acc, rows_buf, hid, pick, place, scale, terms,
     outs, core_in, x_out, x_in, z_out, z_in,
     w_sem, meta_send, meta_recv, z_send, x_send, core_send, tok_recv,
     rc_send, rc_recv, rx_send, rx_recv, rz_send, rz_recv,
@@ -123,12 +124,19 @@
     core_e = 2 * x + 1 - c
     x_e = 2 * (1 - x) + c
     diag_e = 2 * (1 - x) + 1 - c
-    zs = pair_steps(z)
+    zs = near_to_far(z)
+    outer, inner = zs[1], 3 - z
+    middle = z % 3 > 0
+    end = z % 3 == 0
     tok, width = tok_in.shape
     slots = pick.shape[0]
     every = pick.shape[1]
     hidden = hid.shape[1]
 
+    named = lax.broadcasted_iota(jnp.int32, (8, tok), 0)
+    meta_in[...] = jnp.where(routes_in[0:1, :] == named, gates_in[0:1, :], 0.0) + jnp.where(
+        routes_in[1:2, :] == named, gates_in[1:2, :], 0.0
+    )
     weight_copies = []
     for k in range(4):
         cut = pl.ds(pl.multiple_of(zs[k] * width, width), width)
@@ -148,19 +156,29 @@
     barrier = pltpu.get_barrier_semaphore()
     for other in (core_e, x_e, diag_e):
         pl.semaphore_signal(barrier, inc=1, device_id={"expert": other}, device_id_type=MESH)
-    for k in (1, 2, 3):
-        pl.semaphore_signal(barrier, inc=1, device_id={"tensor": zs[k]}, device_id_type=MESH)
-    pl.semaphore_wait(barrier, 6)
+    pl.semaphore_signal(barrier, inc=1, device_id={"tensor": outer}, device_id_type=MESH)
+
+    @pl.when(middle)
+    def _():
+        pl.semaphore_signal(barrier, inc=1, device_id={"tensor": inner}, device_id_type=MESH)
+        pl.semaphore_wait(barrier, 5)
+
+    @pl.when(end)
+    def _():
+        pl.semaphore_wait(barrier, 4)
+
 
     sends = []
 
-    def send(src, dst, s_sem, r_sem, where):
+    def send(src, dst, s_sem, r_sem, where, keep=True):
         copy = pltpu.make_async_remote_copy(
             src_ref=src, dst_ref=dst, send_sem=s_sem, recv_sem=r_sem,
             device_id=where, device_id_type=MESH,
         )
         copy.start()
-        sends.append(copy)
+        if keep:
+            sends.append(copy)
+        return copy
 
     def arrival(ref, sem):
         pltpu.make_async_copy(ref, ref, sem).wait()
@@ -169,15 +187,34 @@
         send(meta_in, meta.at[e], meta_send.at[i], meta_recv.at[e], {"expert": other})
     own = z * 4 + e
     send(tok_in, toks.at[own], x_send.at[0], tok_recv.at[own], {"expert": x_e})
-    for k in (1, 2, 3):
-        send(tok_in, toks.at[own], z_send.at[k - 1], tok_recv.at[own], {"tensor": zs[k]})
+    send(tok_in, toks.at[own], z_send.at[0], tok_recv.at[own], {"tensor": outer})
+
+    @pl.when(middle)
+    def _():
+        send(tok_in, toks.at[own], z_send.at[1], tok_recv.at[own], {"tensor": inner}, False)
+
     send(tok_in, toks.at[own], core_send.at[0], tok_recv.at[own], {"expert": core_e})
     toks[own] = tok_in[...]
     meta[e] = meta_in[...]
 
-    def forward_z(k):
-        block = zs[k] * 4 + e
+    def block_of(k):
+        return zs[k] * 4 + e
+
+    def land_z(k):
+        block = block_of(k)
         arrival(toks.at[block], tok_recv.at[block])
+
+    def pass_on(k):
+        block = block_of(k)
+        there = inner if k == 1 else outer
+        return pltpu.make_async_remote_copy(
+            src_ref=toks.at[block], dst_ref=toks.at[block],
+            send_sem=z_send.at[k + 1], recv_sem=tok_recv.at[block],
+            device_id={"tensor": there}, device_id_type=MESH,
+        )
+
+    def spread_z(k):
+        block = block_of(k)
         send(toks.at[block], toks.at[block], x_send.at[k], tok_recv.at[block], {"expert": x_e})
         send(toks.at[block], toks.at[block], core_send.at[k], tok_recv.at[block], {"expert": core_e})
 
@@ -245,12 +282,44 @@
             block = zs[k] * 4 + other
             arrival(toks.at[block], tok_recv.at[block])
 
-    for k in range(4):
-        if k < 3:
-            forward_z(k + 1)
-        forward_x(k)
-        core_arrivals(k)
-        up_step(k)
+    land_z(1)
+
+    @pl.when(middle)
+    def _():
+        pass_on(1).start()
+        land_z(2)
+        pass_on(2).start()
+
+    spread_z(1)
+    forward_x(0)
+    core_arrivals(0)
+    up_step(0)
+
+    @pl.when(middle)
+    def _():
+        land_z(3)
+        pass_on(3).start()
+
+    @pl.when(end)
+    def _():
+        land_z(2)
+
+    spread_z(2)
+    forward_x(1)
+    core_arrivals(1)
+    up_step(1)
+
+    @pl.when(end)
+    def _():
+        land_z(3)
+
+    spread_z(3)
+    forward_x(2)
+    core_arrivals(2)
+    up_step(2)
+    forward_x(3)
+    core_arrivals(3)
+    up_step(3)
 
     down_tile = 256
 
@@ -286,14 +355,29 @@
             + core_in[k, 1].astype(jnp.float32)
             + x_in[k].astype(jnp.float32)
         )
-        if k > 0:
-            z_out[k - 1] = total.astype(jnp.bfloat16)
+        if k == 0:
+            return total
+
+        def pass_sum(value, slot, there):
+            z_out[k - 1] = value.astype(jnp.bfloat16)
             send(
-                z_out.at[k - 1], z_in.at[k - 1], rz_send.at[k - 1], rz_recv.at[k - 1],
-                {"tensor": zs[k]},
+                z_out.at[k - 1], z_in.at[slot], rz_send.at[k - 1], rz_recv.at[slot],
+                {"tensor": there}, False,
             )
-            return None
-        return total
+
+        @pl.when(end)
+        def _():
+            pass_sum(total, 3 - k, outer)
+
+        @pl.when(middle)
+        def _():
+            pass_sum(total + landed(3 if k == 1 else 3 - k), 6 - k, outer if k == 1 else inner)
+
+        return None
+
+    def landed(slot):
+        arrival(z_in.at[slot], rz_recv.at[slot])
+        return z_in[slot].astype(jnp.float32)
 
     down_step(3)
     core_step(3)
@@ -302,15 +386,25 @@
     x_step(3)
     down_step(1)
     core_step(1)
+    x_step(2)
     down_step(0)
     core_step(0)
-    x_step(2)
     x_step(1)
     total = x_step(0)
-    for k in (3, 2, 1):
-        arrival(z_in.at[k - 1], rz_recv.at[k - 1])
-        total = total + z_in[k - 1].astype(jnp.float32)
-    out[...] = total.astype(jnp.bfloat16)
+
+    @pl.when(end)
+    def _():
+        out[...] = (total + landed(5)).astype(jnp.bfloat16)
+
+    @pl.when(middle)
+    def _():
+        out[...] = (total + landed(2) + landed(4)).astype(jnp.bfloat16)
+        pltpu.make_async_copy(tok_in, tok_in, z_send.at[1]).wait()
+        for k in (1, 2, 3):
+            pltpu.make_async_copy(tok_in, tok_in, z_send.at[k + 1]).wait()
+
+    for k in (1, 2, 3):
+        pltpu.make_async_copy(z_out.at[k - 1], z_out.at[k - 1], rz_send.at[k - 1]).wait()
     for copy in sends:
         copy.wait_send()
 
@@ -322,20 +416,17 @@
     slots = experts * CAP
     padded = (slots + 127) // 128 * 128
     every = experts * tok
-    named = jnp.arange(8, dtype=jnp.int32)[:, None]
-    meta = jnp.where(routes[:, 0][None] == named, gates[:, 0][None], 0.0) + jnp.where(
-        routes[:, 1][None] == named, gates[:, 1][None], 0.0
-    )
     vmem = pl.BlockSpec(memory_space=pltpu.VMEM)
     hbm = pl.BlockSpec(memory_space=pl.ANY)
     bf, f32, dma = jnp.bfloat16, jnp.float32, pltpu.SemaphoreType.DMA
     return pl.pallas_call(
         layer_kernel,
         out_shape=jax.ShapeDtypeStruct((tok, width), bf),
-        in_specs=[vmem, vmem, hbm, hbm, hbm],
+        in_specs=[vmem, vmem, vmem, hbm, hbm, hbm],
         out_specs=vmem,
         scratch_shapes=[
             pltpu.VMEM((4 * experts, tok, width), bf),
+            pltpu.VMEM((8, tok), f32),
             pltpu.VMEM((experts, 8, tok), f32),
             pltpu.VMEM((4, width, hidden), bf),
             pltpu.VMEM((4, width, hidden), bf),
@@ -353,10 +444,10 @@
             pltpu.VMEM((4, tok, width), bf),
             pltpu.VMEM((4, tok, width), bf),
             pltpu.VMEM((3, tok, width), bf),
-            pltpu.VMEM((3, tok, width), bf),
-            dma((12,)), dma((3,)), dma((experts,)), dma((3,)), dma((4,)), dma((8,)),
+            pltpu.VMEM((6, tok, width), bf),
+            dma((12,)), dma((3,)), dma((experts,)), dma((5,)), dma((4,)), dma((8,)),
             dma((4 * experts,)),
-            dma((8,)), dma((8,)), dma((4,)), dma((4,)), dma((3,)), dma((3,)),
+            dma((8,)), dma((8,)), dma((4,)), dma((4,)), dma((3,)), dma((6,)),
         ],
         compiler_params=pltpu.CompilerParams(
             collective_id=0, has_side_effects=True, vmem_limit_bytes=62 * 1024 * 1024
@@ -366,7 +457,7 @@
             bytes_accessed=6 * model * hidden,
             transcendentals=slots * hidden,
         ),
-    )(meta, tokens, w_gate[0], w_up[0], w_down[0])
+    )(routes.T, gates.T, tokens, w_gate[0], w_up[0], w_down[0])
 
 
 def solution(mesh):

time: 68.6 us -> 67.7 us (0.987)
  local copies, waits for them, and re-layouts: 3.13 us -> 1.62 us
  Pallas kernels: 64.6 us -> 65.9 us
    pallas_call x1, Pallas kernels: 64.6 us -> 65.9 us  [per_device_fused(): pl.pallas_call(layer_kernel, out_shape=jax.ShapeDtypeStruct((tok, width),...]
    broadcast_in_dim x1 -> x0, local copies, waits for them, and re-layouts: 0.76 us -> none  [per_device_fused(): jnp.where(routes[:, 0][None] == named, gates[:, 0][None], 0.0)]
    eq x1 -> x0, local copies, waits for them, and re-layouts: 0.76 us -> none  [per_device_fused(): routes[:, 0][None] == named]
where the time goes in v2:
time: 67.7 us; the launch traced here: 67.6 us
  Pallas kernels  65.9 us (97%)
  local copies, waits for them, and re-layouts  1.62 us (2%)
    pallas_call x1, Pallas kernels, per_device_fused(): pl.pallas_call(layer_kernel, out_shape=jax.ShapeDtypeStruct((tok, width),...  65.9 us
    unnamed x1, local copies, waits for them, and re-layouts  1.62 us

profile of v2, /device:TPU:0, one launch (start us, length us, event | category | flops | bytes accessed | tf_op | source)
XLA Modules:
  0.0 67.6 jit_solution(5232714234646341397)
XLA Ops:
  0.0 65.9 %shard_map.64 = bf16[128,768]{1,0:T(8,128)(2,1)} custom-call(s32[2,128]{1,0:T(2,128)} %bitcast.8, f32[2,128]{1,0:T(2,128)} %bitcast.9, bf16[128,768]{1,0:T(8,128)(2,1)} %tok_in.1, bf16[3072,2048]{1,0:T(8,128)(2,1)} %bitcast.5, bf16[3072,2048]{1,0:T(8,128)(2,1)} %bitcast.6, bf16[2048,3072]{1,0:T(8,128)(2,1)} %bitcast.7), custom_call_target="tpu_custom_call" | custom-call | flops 10871635968 | bytes 37748736 | tf_op jit(solution)/shard_map/pallas_call | solution.py:422
  65.9 1.6 %copy.8 = bf16[128,768]{1,0:T(8,128)(2,1)} copy(bf16[128,768]{1,0:T(8,128)(2,1)} %shard_map.64) | data formatting | bytes 393216

commit v3 on v2

--- a/solution.py
+++ b/solution.py
@@ -185,43 +185,50 @@
 
     for i, other in enumerate((x_e, core_e, diag_e)):
         send(meta_in, meta.at[e], meta_send.at[i], meta_recv.at[e], {"expert": other})
-    own = z * 4 + e
-    send(tok_in, toks.at[own], x_send.at[0], tok_recv.at[own], {"expert": x_e})
-    send(tok_in, toks.at[own], z_send.at[0], tok_recv.at[own], {"tensor": outer})
-
-    @pl.when(middle)
-    def _():
-        send(tok_in, toks.at[own], z_send.at[1], tok_recv.at[own], {"tensor": inner}, False)
-
-    send(tok_in, toks.at[own], core_send.at[0], tok_recv.at[own], {"expert": core_e})
-    toks[own] = tok_in[...]
+    half = tok // 2
+    own = 2 * (z * 4 + e)
+
+    def own_half(h):
+        return tok_in.at[pl.ds(h * half, half)]
+
+    for h in (0, 1):
+        send(own_half(h), toks.at[own + h], x_send.at[h], tok_recv.at[own + h], {"expert": x_e})
+        send(own_half(h), toks.at[own + h], z_send.at[h], tok_recv.at[own + h], {"tensor": outer})
+
+        @pl.when(middle)
+        def _():
+            send(
+                own_half(h), toks.at[own + h], z_send.at[2 + h], tok_recv.at[own + h],
+                {"tensor": inner}, False,
+            )
+
+        send(own_half(h), toks.at[own + h], core_send.at[h], tok_recv.at[own + h], {"expert": core_e})
+    toks[own] = tok_in[0:half, :]
+    toks[own + 1] = tok_in[half:, :]
     meta[e] = meta_in[...]
 
-    def block_of(k):
-        return zs[k] * 4 + e
-
-    def land_z(k):
-        block = block_of(k)
-        arrival(toks.at[block], tok_recv.at[block])
-
-    def pass_on(k):
-        block = block_of(k)
-        there = inner if k == 1 else outer
-        return pltpu.make_async_remote_copy(
-            src_ref=toks.at[block], dst_ref=toks.at[block],
-            send_sem=z_send.at[k + 1], recv_sem=tok_recv.at[block],
-            device_id={"tensor": there}, device_id_type=MESH,
-        )
-
-    def spread_z(k):
-        block = block_of(k)
-        send(toks.at[block], toks.at[block], x_send.at[k], tok_recv.at[block], {"expert": x_e})
-        send(toks.at[block], toks.at[block], core_send.at[k], tok_recv.at[block], {"expert": core_e})
+    def piece_of(k, other, h):
+        return 2 * (zs[k] * 4 + other) + h
+
+    def land(k, other, h):
+        piece = piece_of(k, other, h)
+        arrival(toks.at[piece], tok_recv.at[piece])
+
+    def hand_on(k, other, h, sem, where, keep=True):
+        piece = piece_of(k, other, h)
+        send(toks.at[piece], toks.at[piece], sem, tok_recv.at[piece], where, keep)
+
+    def spread_z(k, h):
+        hand_on(k, e, h, x_send.at[2 * k + h], {"expert": x_e})
+        hand_on(k, e, h, core_send.at[2 * k + h], {"expert": core_e})
+
+    def pass_on(k, h):
+        hand_on(k, e, h, z_send.at[2 * (k + 1) + h], {"tensor": inner if k == 1 else outer}, False)
 
     def forward_x(k):
-        block = zs[k] * 4 + x_e
-        arrival(toks.at[block], tok_recv.at[block])
-        send(toks.at[block], toks.at[block], core_send.at[4 + k], tok_recv.at[block], {"expert": core_e})
+        for h in (0, 1):
+            land(k, x_e, h)
+            hand_on(k, x_e, h, core_send.at[8 + 2 * k + h], {"expert": core_e})
 
     for other in (x_e, core_e, diag_e):
         arrival(meta.at[other], meta_recv.at[other])
@@ -257,7 +264,7 @@
     def up_step(k):
         weight_copies[k][0].wait()
         weight_copies[k][1].wait()
-        blocks = toks[pl.ds(zs[k] * 4, 4)].reshape(every, width)
+        blocks = toks[pl.ds(zs[k] * 8, 8)].reshape(every, width)
         rows_buf[...] = jnp.dot(
             pick[...], blocks, preferred_element_type=jnp.float32
         ).astype(jnp.bfloat16)
@@ -279,41 +286,54 @@
 
     def core_arrivals(k):
         for other in (core_e, diag_e):
-            block = zs[k] * 4 + other
-            arrival(toks.at[block], tok_recv.at[block])
-
-    land_z(1)
+            for h in (0, 1):
+                land(k, other, h)
+
+    def relay(k, passing):
+        for h in (0, 1):
+            land(k, e, h)
+            if passing:
+                pass_on(k, h)
+
+    for h in (0, 1):
+        land(1, e, h)
+
+        @pl.when(middle)
+        def _():
+            pass_on(1, h)
+
+        spread_z(1, h)
 
     @pl.when(middle)
     def _():
-        pass_on(1).start()
-        land_z(2)
-        pass_on(2).start()
-
-    spread_z(1)
+        relay(2, True)
+
     forward_x(0)
     core_arrivals(0)
     up_step(0)
+    for h in (0, 1):
+
+        @pl.when(end)
+        def _():
+            land(2, e, h)
+
+        spread_z(2, h)
 
     @pl.when(middle)
     def _():
-        land_z(3)
-        pass_on(3).start()
-
-    @pl.when(end)
-    def _():
-        land_z(2)
-
-    spread_z(2)
+        relay(3, True)
+
     forward_x(1)
     core_arrivals(1)
     up_step(1)
-
-    @pl.when(end)
-    def _():
-        land_z(3)
-
-    spread_z(3)
+    for h in (0, 1):
+
+        @pl.when(end)
+        def _():
+            land(3, e, h)
+
+        spread_z(3, h)
+
     forward_x(2)
     core_arrivals(2)
     up_step(2)
@@ -340,71 +360,80 @@
                 rc_send.at[2 * k + i], rc_recv.at[2 * k + i], {"expert": core_e},
             )
 
+    def cut(h):
+        return pl.ds(h * half, half)
+
+    def wide(value):
+        return value.astype(jnp.float32)
+
     def core_step(k):
         arrival(core_in.at[k, 0], rc_recv.at[2 * k])
-        x_out[k] = (
-            outs[k, x_e].astype(jnp.float32) + core_in[k, 0].astype(jnp.float32)
-        ).astype(jnp.bfloat16)
-        send(x_out.at[k], x_in.at[k], rx_send.at[k], rx_recv.at[k], {"expert": x_e})
+        for h in (0, 1):
+            x_out[k, cut(h)] = (wide(outs[k, x_e, cut(h)]) + wide(core_in[k, 0, cut(h)])).astype(
+                jnp.bfloat16
+            )
+            send(
+                x_out.at[k, cut(h)], x_in.at[k, cut(h)], rx_send.at[2 * k + h],
+                rx_recv.at[2 * k + h], {"expert": x_e},
+            )
+
+    def landed(slot, h):
+        arrival(z_in.at[slot, cut(h)], rz_recv.at[2 * slot + h])
+        return wide(z_in[slot, cut(h)])
 
     def x_step(k):
         arrival(core_in.at[k, 1], rc_recv.at[2 * k + 1])
-        arrival(x_in.at[k], rx_recv.at[k])
-        total = (
-            outs[k, e].astype(jnp.float32)
-            + core_in[k, 1].astype(jnp.float32)
-            + x_in[k].astype(jnp.float32)
-        )
-        if k == 0:
-            return total
-
-        def pass_sum(value, slot, there):
-            z_out[k - 1] = value.astype(jnp.bfloat16)
-            send(
-                z_out.at[k - 1], z_in.at[slot], rz_send.at[k - 1], rz_recv.at[slot],
-                {"tensor": there}, False,
+        for h in (0, 1):
+            arrival(x_in.at[k, cut(h)], rx_recv.at[2 * k + h])
+            total = (
+                wide(outs[k, e, cut(h)]) + wide(core_in[k, 1, cut(h)]) + wide(x_in[k, cut(h)])
             )
 
-        @pl.when(end)
-        def _():
-            pass_sum(total, 3 - k, outer)
-
-        @pl.when(middle)
-        def _():
-            pass_sum(total + landed(3 if k == 1 else 3 - k), 6 - k, outer if k == 1 else inner)
-
-        return None
-
-    def landed(slot):
-        arrival(z_in.at[slot], rz_recv.at[slot])
-        return z_in[slot].astype(jnp.float32)
+            def pass_sum(value, slot, there):
+                z_out[k - 1, cut(h)] = value.astype(jnp.bfloat16)
+                send(
+                    z_out.at[k - 1, cut(h)], z_in.at[slot, cut(h)], rz_send.at[2 * (k - 1) + h],
+                    rz_recv.at[2 * slot + h], {"tensor": there}, False,
+                )
+
+            @pl.when(end)
+            def _():
+                if k == 0:
+                    out[cut(h), :] = (total + landed(5, h)).astype(jnp.bfloat16)
+                else:
+                    pass_sum(total, 3 - k, outer)
+
+            @pl.when(middle)
+            def _():
+                if k == 0:
+                    out[cut(h), :] = (total + landed(2, h) + landed(4, h)).astype(jnp.bfloat16)
+                else:
+                    pass_sum(
+                        total + landed(3 if k == 1 else 3 - k, h), 6 - k, outer if k == 1 else inner
+                    )
 
     down_step(3)
+    down_step(2)
     core_step(3)
-    down_step(2)
+    down_step(1)
     core_step(2)
     x_step(3)
-    down_step(1)
+    down_step(0)
     core_step(1)
+    core_step(0)
     x_step(2)
-    down_step(0)
-    core_step(0)
     x_step(1)
-    total = x_step(0)
-
-    @pl.when(end)
-    def _():
-        out[...] = (total + landed(5)).astype(jnp.bfloat16)
+    x_step(0)
 
     @pl.when(middle)
     def _():
-        out[...] = (total + landed(2) + landed(4)).astype(jnp.bfloat16)
-        pltpu.make_async_copy(tok_in, tok_in, z_send.at[1]).wait()
-        for k in (1, 2, 3):
-            pltpu.make_async_copy(tok_in, tok_in, z_send.at[k + 1]).wait()
-
-    for k in (1, 2, 3):
-        pltpu.make_async_copy(z_out.at[k - 1], z_out.at[k - 1], rz_send.at[k - 1]).wait()
+        for i in range(2, 10):
+            pltpu.make_async_copy(own_half(0), own_half(0), z_send.at[i]).wait()
+
+    for i in range(6):
+        sent = z_out.at[i // 2, cut(i % 2)]
+        pltpu.make_async_copy(sent, sent, rz_send.at[i]).wait()
+
     for copy in sends:
         copy.wait_send()
 
@@ -425,7 +454,7 @@
         in_specs=[vmem, vmem, vmem, hbm, hbm, hbm],
         out_specs=vmem,
         scratch_shapes=[
-            pltpu.VMEM((4 * experts, tok, width), bf),
+            pltpu.VMEM((8 * experts, tok // 2, width), bf),
             pltpu.VMEM((8, tok), f32),
             pltpu.VMEM((experts, 8, tok), f32),
             pltpu.VMEM((4, width, hidden), bf),
@@ -445,9 +474,9 @@
             pltpu.VMEM((4, tok, width), bf),
             pltpu.VMEM((3, tok, width), bf),
             pltpu.VMEM((6, tok, width), bf),
-            dma((12,)), dma((3,)), dma((experts,)), dma((5,)), dma((4,)), dma((8,)),
-            dma((4 * experts,)),
-            dma((8,)), dma((8,)), dma((4,)), dma((4,)), dma((3,)), dma((6,)),
+            dma((12,)), dma((3,)), dma((experts,)), dma((10,)), dma((8,)), dma((16,)),
+            dma((8 * experts,)),
+            dma((8,)), dma((8,)), dma((8,)), dma((8,)), dma((6,)), dma((12,)),
         ],
         compiler_params=pltpu.CompilerParams(
             collective_id=0, has_side_effects=True, vmem_limit_bytes=62 * 1024 * 1024

time: 67.7 us -> 63.9 us (0.944)
  Pallas kernels: 65.9 us -> 62.1 us
    pallas_call x1, Pallas kernels: 65.9 us -> 62.1 us  [per_device_fused(): pl.pallas_call(layer_kernel, out_shape=jax.ShapeDtypeStruct((tok, width),...]
where the time goes in v3:
time: 63.9 us; the launch traced here: 63.8 us
  Pallas kernels  62.1 us (97%)
  local copies, waits for them, and re-layouts  1.62 us (3%)
    pallas_call x1, Pallas kernels, per_device_fused(): pl.pallas_call(layer_kernel, out_shape=jax.ShapeDtypeStruct((tok, width),...  62.1 us
    unnamed x1, local copies, waits for them, and re-layouts  1.62 us

profile of v3, /device:TPU:0, one launch (start us, length us, event | category | flops | bytes accessed | tf_op | source)
XLA Modules:
  0.0 63.8 jit_solution(18151376963304228477)
XLA Ops:
  0.0 62.1 %shard_map.64 = bf16[128,768]{1,0:T(8,128)(2,1)} custom-call(s32[2,128]{1,0:T(2,128)} %bitcast.8, f32[2,128]{1,0:T(2,128)} %bitcast.9, bf16[128,768]{1,0:T(8,128)(2,1)} %tok_in.1, bf16[3072,2048]{1,0:T(8,128)(2,1)} %bitcast.5, bf16[3072,2048]{1,0:T(8,128)(2,1)} %bitcast.6, bf16[2048,3072]{1,0:T(8,128)(2,1)} %bitcast.7), custom_call_target="tpu_custom_call" | custom-call | flops 10871635968 | bytes 37748736 | tf_op jit(solution)/shard_map/pallas_call | solution.py:451
  62.1 1.6 %copy.8 = bf16[128,768]{1,0:T(8,128)(2,1)} copy(bf16[128,768]{1,0:T(8,128)(2,1)} %shard_map.64) | data formatting | bytes 393216
